TPU v7x, 32 devices: a whole 2x2x4 slice. The times are simulated.
32 devices in a mesh: tok: 4 (over x, core), hid: 8 (over z, y).
Axes of the slice: x: 2, y: 2, z: 4, core: 2. Of those that a mesh axis runs over, the one named last changes fastest.
Arguments:
- gate_pre: bfloat16 [512, 24576], P('tok', 'hid'), may hold values from -6 to 6
- up_pre: bfloat16 [512, 24576], P('tok', 'hid'), may hold values from -6 to 6
- down_weight: bfloat16 [24576, 6144], P('hid', 'tok'), may hold values from -0.0546875 to 0.0546875
- residual: bfloat16 [512, 6144], P('tok', 'hid'), may hold values from -3 to 3
Outputs:
- mixed: bfloat16 [512, 6144], P('tok', 'hid')
All inputs are finite; a program needn't handle non-finite values.
Results may differ from a plain program's by a relative error of at most 0.0043.
Values may be sent and summed in bfloat16 or wider, within the bound.
A program may use at most 64 MiB of HBM per device.

v0:
```python
import jax
import jax.numpy as jnp
from jax import lax
from jax.sharding import PartitionSpec as P


def hidden_total(partial_value):
    return lax.psum_scatter(partial_value, "hid", scatter_dimension=1, tiled=True)


def per_device(gate_pre, up_pre, down_weight, residual):
    hidden = (jax.nn.silu(gate_pre.astype(jnp.float32)) * up_pre.astype(jnp.float32)).astype(
        jnp.bfloat16
    )
    every_token = jnp.dot(
        lax.all_gather(hidden, "tok", axis=0, tiled=True),
        down_weight,
        preferred_element_type=jnp.float32,
    )
    partial_value = lax.all_to_all(every_token, "tok", split_axis=0, concat_axis=1, tiled=True)
    summed = hidden_total(partial_value)
    return (summed + residual.astype(jnp.float32)).astype(jnp.bfloat16)


def solution(mesh):
    in_specs = (P("tok", "hid"), P("tok", "hid"), P("hid", "tok"), P("tok", "hid"))
    out_specs = P("tok", "hid")
    return jax.shard_map(
        per_device, mesh=mesh, in_specs=in_specs, out_specs=out_specs, check_vma=False
    )
```

profile of v0, /device:TPU:0, one launch (start us, length us, event | category | flops | bytes accessed | tf_op | source)
XLA Modules:
  0.0 173.7 jit_solution(4540382244615017929)
XLA Ops:
  6.5 0.0 all-gather.2.cloned.1.call-start
  6.5 2.7 %fusion.4 = bf16[128,3072]{1,0:T(8,128)(2,1)} fusion(bf16[128,3072]{1,0:T(8,128)(2,1)} %param.5, bf16[128,3072]{1,0:T(8,128)(2,1)} %param.4), kind=kLoop, calls=%fused_computation.6 | loop fusion | flops 3145728 | bytes 2359296 | tf_op jit(solution)/shard_map/convert_element_type | solution.py:12
  9.3 0.0 all-gather.2.cloned.1.call-update
  9.3 0.0 reduce-scatter.2.cloned.1.call-start
  9.3 31.3 %all-gather.2.cloned.1.call-done = bf16[512,3072]{1,0:T(8,128)(2,1)} async-done(((bf16[128,3072]{1,0:T(8,128)(2,1)}), bf16[512,3072]{1,0:T(8,128)(2,1)}) %all-gather.2.cloned.1.call-update) | async-done | bytes 3145744 | tf_op jit(solution)/shard_map/all_gather | solution.py:16
  40.7 8.6 %fusion.5 = f32[512,1536]{1,0:T(8,128)S(1)} fusion(bf16[512,3072]{1,0:T(8,128)(2,1)} %all-gather.2.cloned.1.call-done, bf16[3072,1536]{1,0:T(8,128)(2,1)} %param.6), kind=kOutput, calls=%fused_computation.8 | convolution fusion | flops 4831838208 | bytes 15728640 | tf_op jit(solution)/shard_map/dot_general | solution.py:15
  49.2 39.4 %all_to_all.19 = f32[4,128,1536]{2,1,0:T(8,128)S(1)} all-to-all(f32[4,128,1536]{2,1,0:T(8,128)S(1)} %bitcast.8), channel_id=1, replica_groups=mesh['tok'=4,'hid'=8] {'tok'}, dimensions={0} | all-to-all | bytes 6291456 | tf_op jit(solution)/shard_map/all_to_all | solution.py:20
  88.7 1.8 %copy.6 = f32[4,16,8,1536]{3,2,0,1:T(8,128)} copy(f32[4,16,8,1536]{3,2,1,0:T(8,128)S(1)} %bitcast.7) | data formatting | bytes 6291456 | tf_op jit(solution)/shard_map/all_to_all | solution.py:20
  90.5 0.0 copy-start
  90.5 0.0 reduce-scatter.2.cloned.1.call-update
  90.6 74.6 %reduce-scatter.2.cloned.1.call-done = f32[128,768]{1,0:T(8,128)} async-done(((f32[128,6144]{1,0:T(8,128)}), f32[128,768]{1,0:T(8,128)}) %reduce-scatter.2.cloned.1.call-update) | async-done | bytes 393232 | tf_op jit(solution)/shard_map/reduce_scatter | solution.py:8
  165.1 0.0 copy-done
  165.1 1.7 add_convert_fusion
Async XLA Ops:
  6.5 34.1 %all-gather.2.cloned.1.call-start = ((), (), s32[]{:S(2)}) async-start(), calls=%async_computation.2 | async-start | bytes 3932160 | tf_op jit(solution)/shard_map/all_gather | solution.py:16
  9.3 155.9 %reduce-scatter.2.cloned.1.call-start = ((), (), s32[]{:S(2)}) async-start(), calls=%async_computation.3 | async-start | bytes 3538944 | tf_op jit(solution)/shard_map/reduce_scatter | solution.py:8
  90.5 74.6 %copy-start = (bf16[128,768]{1,0:T(8,128)(2,1)S(1)}, bf16[128,768]{1,0:T(8,128)(2,1)}, u32[]{:S(2)}) copy-start(bf16[128,768]{1,0:T(8,128)(2,1)} %param.7) | copy-start | bytes 589828
Sparse Core Ops, SparseCore 0:
  9.4 31.2 all-gather.1
  90.7 74.4 reduce-scatter.1
where the time goes:
time: 174 us
  waiting for transfers between devices  106 us (61%)
  blocking collectives  39.4 us (23%)
  between operations  13.4 us (8%)
  matrix products  8.56 us (5%)
  other arithmetic  4.42 us (3%)
  local copies, waits for them, and re-layouts  1.85 us (1%)
    reduce_scatter x1, waiting for transfers between devices, hidden_total(): lax.psum_scatter(partial_value, 'hid', scatter_dimension=1, tiled=True)  74.6 us
    all_to_all x1, blocking collectives, per_device(): lax.all_to_all(every_token, 'tok', split_axis=0, concat_axis=1, tiled=True)  39.4 us
    all_gather x1, waiting for transfers between devices, per_device(): lax.all_gather(hidden, 'tok', axis=0, tiled=True)  31.3 us
    dot_general x1, matrix products, per_device(): jnp.dot(lax.all_gather(hidden, 'tok', axis=0, tiled=True), down_weight, p...  8.56 us
  transfers between devices with their start and end apart: 2, of which 2 were waited for; matrix products, arithmetic and copies ran while one was open for 0% of the time, Pallas kernels for 0%

commit v1 on v0

v1 whole, which is shorter than its diff:
```python
import jax
import jax.numpy as jnp
from jax import lax
from jax.experimental import pallas as pl
from jax.experimental.pallas import tpu as pltpu
from jax.sharding import PartitionSpec as P

MESH = pl.DeviceIdType.MESH
ROWS = 32
TILE = 256
F32, BF16 = jnp.float32, jnp.bfloat16


def collective_form(gate_pre, up_pre, down_weight, residual):
    hidden = (jax.nn.silu(gate_pre.astype(F32)) * up_pre.astype(F32)).astype(BF16)
    every_token = jnp.dot(
        lax.all_gather(hidden, "tok", axis=0, tiled=True),
        down_weight,
        preferred_element_type=F32,
    )
    partial_value = lax.all_to_all(every_token, "tok", split_axis=0, concat_axis=1, tiled=True)
    summed = lax.psum_scatter(partial_value, "hid", scatter_dimension=1, tiled=True)
    return (summed + residual.astype(F32)).astype(BF16)


def kernel(
    gate, up, weight, out,
    gbuf, ubuf, wbuf, hbuf, acc, ysend, yrecv, zsend, zrecv, fsend, land,
    gsem, usem, wsem, xs, xr, cs, cr, ls, lr, ys, yr, zs, zr, fs, fr,
):
    nk, rows, ff = gbuf.shape
    ng, _, half = acc.shape
    t, h = lax.axis_index("tok"), lax.axis_index("hid")
    x, c = lax.div(t, 2), lax.rem(t, 2)
    z, y = lax.div(h, 2), lax.rem(h, 2)
    z1, z0 = lax.div(z, 2), lax.rem(z, 2)
    gathers = z0 == c
    core_t, x_t = 2 * x + 1 - c, 2 * (1 - x) + c
    y_h, z_h = 2 * z + 1 - y, 2 * (2 * z1 + 1 - z0) + y

    def load(k, source, buf, sem):
        return pltpu.make_async_copy(source.at[pl.ds(k * rows, rows)], buf.at[k], sem.at[k])

    def load_weight(which):
        columns = pl.ds(pl.multiple_of((1 - y if which == 0 else y) * half, 128), half)
        return pltpu.make_async_copy(weight.at[:, columns], wbuf.at[which], wsem.at[which])

    def remote(src, dst, send, recv, tok, hid):
        return pltpu.make_async_remote_copy(
            src_ref=src, dst_ref=dst, send_sem=send, recv_sem=recv,
            device_id=(tok, hid), device_id_type=MESH,
        )

    def block(g, core):
        return hbuf.at[g, pl.ds(pl.multiple_of(core * rows, rows), rows)]

    def core_copy(k, core):
        return remote(block(k, core), block(k, core), cs.at[k], cr.at[k], core_t, h)

    def x_copy(k):
        return remote(block(k, c), block(nk + k, c), xs.at[k], xr.at[k], x_t, h)

    def relay(k, core):
        return remote(block(nk + k, core), block(nk + k, core), ls.at[k], lr.at[k], core_t, h)

    def y_copy(g):
        return remote(ysend.at[g], yrecv.at[g], ys.at[g], yr.at[g], t, y_h)

    def z_copy(g):
        return remote(zsend.at[g], zrecv.at[g], zs.at[g], zr.at[g], t, z_h)

    def final_copy(g, core, slot, k, tok):
        return remote(
            fsend.at[g, pl.ds(core * rows, rows)], land.at[slot, k],
            fs.at[g, core], fr.at[slot, k], tok, 2 * t + y,
        )

    for k in range(nk):
        load(k, gate, gbuf, gsem).start()
        load(k, up, ubuf, usem).start()
    load_weight(0).start()
    load_weight(1).start()

    barrier = pltpu.get_barrier_semaphore()

    def greet(tok, hid):
        pl.semaphore_signal(barrier, inc=1, device_id=(tok, hid), device_id_type=MESH)

    greet(core_t, h)
    greet(x_t, h)
    greet(t, y_h)

    @pl.when(gathers)
    def _():
        greet(t, z_h)

    source_h = [2 * (2 * slot + lax.rem(z, 2)) + y for slot in range(2)]
    local_land = [jnp.logical_and(z == t, z1 == slot) for slot in range(2)]
    for slot in range(2):

        @pl.when(jnp.logical_not(local_land[slot]))
        def _():
            greet(z, source_h[slot])

    owners = jnp.where(z == t, 3, 4)
    pl.semaphore_wait(barrier, 3 + jnp.where(gathers, owners, 1))

    wide = 512

    def activate(k, _):
        load(k, gate, gbuf, gsem).wait()
        load(k, up, ubuf, usem).wait()

        def piece(j, _):
            columns = pl.ds(pl.multiple_of(j * wide, wide), wide)
            v = gbuf[k, :, columns].astype(F32)
            u = ubuf[k, :, columns].astype(F32)
            block(k, c)[:, columns] = (v / (1.0 + jnp.exp(-v)) * u).astype(BF16)
            return 0

        lax.fori_loop(0, ff // wide, piece, 0)
        x_copy(k).start()
        core_copy(k, c).start()
        return 0

    lax.fori_loop(0, nk, activate, 0)

    def tiles(step):
        def one(n, _):
            step(pl.ds(pl.multiple_of(n * TILE, TILE), TILE))
            return 0

        lax.fori_loop(0, half // TILE, one, 0)

    def after_y(g):
        y_copy(g).wait_recv()

        @pl.when(gathers)
        def _():
            def step(cols):
                acc[g, :, cols] = acc[g, :, cols] + yrecv[g, :, cols].astype(F32)

            tiles(step)

        @pl.when(jnp.logical_not(gathers))
        def _():
            def step(cols):
                zsend[g, :, cols] = (acc[g, :, cols] + yrecv[g, :, cols].astype(F32)).astype(BF16)

            tiles(step)
            z_copy(g).start()

    def owner_of(g, core):
        chip = jnp.where(g < nk, x, 1 - x)
        tok = 2 * chip + core
        return tok, lax.rem(g, nk), jnp.logical_and(tok == t, z == t)

    def after_z(g):
        @pl.when(gathers)
        def _():
            z_copy(g).wait_recv()

            def step(cols):
                fsend[g, :, cols] = (acc[g, :, cols] + zrecv[g, :, cols].astype(F32)).astype(BF16)

            tiles(step)
            for core in range(2):
                tok, k, local = owner_of(g, core)

                @pl.when(local)
                def _():
                    land[z1, k] = fsend[g, core * rows : (core + 1) * rows]

                @pl.when(jnp.logical_not(local))
                def _():
                    final_copy(g, core, z1, k, tok).start()

    def chunk(g, _):
        @pl.when(jnp.logical_and(g >= nk, g < ng))
        def _():
            x_copy(g - nk).wait_recv()
            relay(g - nk, c).start()

        @pl.when(jnp.logical_and(g >= 1, g <= ng))
        def _():
            after_y(g - 1)

        @pl.when(g >= 2)
        def _():
            after_z(g - 2)

        @pl.when(g < ng)
        def _():
            @pl.when(g < nk)
            def _():
                core_copy(g, 1 - c).wait_recv()

            @pl.when(g >= nk)
            def _():
                relay(g - nk, 1 - c).wait_recv()

            def product(which, cols):
                return jnp.dot(hbuf[g], wbuf[which, :, cols], preferred_element_type=F32)

            @pl.when(g == 0)
            def _():
                load_weight(0).wait()

            def give(cols):
                ysend[g, :, cols] = product(0, cols).astype(BF16)

            tiles(give)
            y_copy(g).start()

            @pl.when(g == 0)
            def _():
                load_weight(1).wait()

            def keep(cols):
                acc[g, :, cols] = product(1, cols)

            tiles(keep)

        return 0

    lax.fori_loop(0, ng + 2, chunk, 0)

    def finish(k, _):
        for slot in range(2):

            @pl.when(jnp.logical_not(local_land[slot]))
            def _():
                final_copy(0, 0, slot, k, core_t).wait_recv()

        span = pl.ds(pl.multiple_of(k * rows, rows), rows)
        out[span, :] = land[0, k].astype(F32) + land[1, k].astype(F32)
        return 0

    lax.fori_loop(0, nk, finish, 0)

    def drain_k(k, _):
        x_copy(k).wait_send()
        core_copy(k, c).wait_send()
        relay(k, c).wait_send()
        return 0

    lax.fori_loop(0, nk, drain_k, 0)

    def drain_g(g, _):
        y_copy(g).wait_send()

        @pl.when(jnp.logical_not(gathers))
        def _():
            z_copy(g).wait_send()

        @pl.when(gathers)
        def _():
            for core in range(2):
                tok, k, local = owner_of(g, core)

                @pl.when(jnp.logical_not(local))
                def _():
                    final_copy(g, core, z1, k, tok).wait_send()

        return 0

    lax.fori_loop(0, ng, drain_g, 0)


def kernel_form(gate_pre, up_pre, down_weight, residual):
    tokens, ff = gate_pre.shape
    half = residual.shape[1]
    rows = ROWS
    nk = tokens // rows
    ng = 2 * nk
    dma = pltpu.SemaphoreType.DMA
    summed = pl.pallas_call(
        kernel,
        out_shape=jax.ShapeDtypeStruct((tokens, half), F32),
        in_specs=[pl.BlockSpec(memory_space=pl.ANY)] * 3,
        out_specs=pl.BlockSpec(memory_space=pltpu.VMEM),
        scratch_shapes=[
            pltpu.VMEM((nk, rows, ff), BF16),
            pltpu.VMEM((nk, rows, ff), BF16),
            pltpu.VMEM((2, ff, half), BF16),
            pltpu.VMEM((ng, 2 * rows, ff), BF16),
            pltpu.VMEM((ng, 2 * rows, half), F32),
        ]
        + [pltpu.VMEM((ng, 2 * rows, half), BF16)] * 5
        + [pltpu.VMEM((2, nk, rows, half), BF16)]
        + [dma((nk,)), dma((nk,)), dma((2,))]
        + [dma((nk,))] * 6
        + [dma((ng,))] * 4
        + [dma((ng, 2)), dma((2, nk))],
        compiler_params=pltpu.CompilerParams(
            collective_id=0, has_side_effects=True, vmem_limit_bytes=50 * 2**20
        ),
        cost_estimate=pl.CostEstimate(
            flops=2 * 4 * tokens * ff * 2 * half,
            bytes_accessed=2 * ff * (2 * half + 2 * tokens),
            transcendentals=tokens * ff,
        ),
    )(gate_pre, up_pre, down_weight)
    return (summed + residual.astype(F32)).astype(BF16)


def solution(mesh):
    in_specs = (P("tok", "hid"), P("tok", "hid"), P("hid", "tok"), P("tok", "hid"))
    out_specs = P("tok", "hid")
    fits = mesh.shape["tok"] == 4 and mesh.shape["hid"] == 8
    return jax.shard_map(
        kernel_form if fits else collective_form,
        mesh=mesh, in_specs=in_specs, out_specs=out_specs, check_vma=False,
    )
```

time: 174 us -> 58.9 us (0.34)
  the two profiles are of different devices: /device:TPU:0 before, /device:TPU:7 now
where the time goes in v1:
time: 58.9 us; the launch traced here: 58.8 us
  Pallas kernels  55.8 us (95%)
  local copies, waits for them, and re-layouts  2.27 us (4%)
  other arithmetic  0.71 us (1%)
    pallas_call x1, Pallas kernels, kernel_form(): pl.pallas_call(kernel, out_shape=jax.ShapeDtypeStruct((tokens, half), F32...  55.8 us
    unnamed x6, local copies, waits for them, and re-layouts  2.27 us

profile of v1, /device:TPU:7, one launch (start us, length us, event | category | flops | bytes accessed | tf_op | source)
XLA Modules:
  0.0 58.8 jit_solution(855879305662786325)
XLA Ops:
  0.0 0.0 copy-start
  0.0 1.1 %copy-done = bf16[128,3072]{1,0:T(8,128)(2,1)S(1)} copy-done((bf16[128,3072]{1,0:T(8,128)(2,1)S(1)}, bf16[128,3072]{1,0:T(8,128)(2,1)}, u32[]{:S(2)}) %copy-start) | copy-done | bytes 786456
  1.1 0.0 copy-start.1
  1.1 1.1 %copy-done.1 = bf16[128,3072]{1,0:T(8,128)(2,1)S(1)} copy-done((bf16[128,3072]{1,0:T(8,128)(2,1)S(1)}, bf16[128,3072]{1,0:T(8,128)(2,1)}, u32[]{:S(2)}) %copy-start.1) | copy-done | bytes 786456
  2.3 0.0 copy-start.2
  2.3 55.8 %shard_map.46 = f32[128,768]{1,0:T(8,128)S(1)} custom-call(bf16[128,3072]{1,0:T(8,128)(2,1)S(1)} %copy-done, bf16[128,3072]{1,0:T(8,128)(2,1)S(1)} %copy-done.1, bf16[3072,1536]{1,0:T(8,128)(2,1)} %weight.1), custom_call_target="tpu_custom_call" | custom-call | flops 4831838208 | bytes 11010048 | tf_op jit(solution)/shard_map/pallas_call | solution.py:277
  58.0 0.0 copy-done.2
  58.0 0.7 %add_convert_fusion = bf16[128,768]{1,0:T(8,128)(2,1)} fusion(f32[128,768]{1,0:T(8,128)S(1)} %shard_map.46, bf16[128,768]{1,0:T(8,128)(2,1)S(1)} %copy-done.2), kind=kLoop, calls=%fused_computation | loop fusion | flops 294912 | bytes 786432 | tf_op jit(solution)/shard_map/convert_element_type | solution.py:304
Async XLA Ops:
  0.0 1.1 %copy-start = (bf16[128,3072]{1,0:T(8,128)(2,1)S(1)}, bf16[128,3072]{1,0:T(8,128)(2,1)}, u32[]{:S(2)}) copy-start(bf16[128,3072]{1,0:T(8,128)(2,1)} %gate.1) | copy-start | bytes 2359300
  1.1 1.1 %copy-start.1 = (bf16[128,3072]{1,0:T(8,128)(2,1)S(1)}, bf16[128,3072]{1,0:T(8,128)(2,1)}, u32[]{:S(2)}) copy-start(bf16[128,3072]{1,0:T(8,128)(2,1)} %up.1) | copy-start | bytes 2359300
  2.3 55.8 %copy-start.2 = (bf16[128,768]{1,0:T(8,128)(2,1)S(1)}, bf16[128,768]{1,0:T(8,128)(2,1)}, u32[]{:S(2)}) copy-start(bf16[128,768]{1,0:T(8,128)(2,1)} %param.7) | copy-start | bytes 589828

commit v2 on v0

v2 whole, which is shorter than its diff:
```python
import jax
import jax.numpy as jnp
from jax import lax
from jax.experimental import pallas as pl
from jax.experimental.pallas import tpu as pltpu
from jax.sharding import PartitionSpec as P

MESH = pl.DeviceIdType.MESH
ROWS = 32
TILE = 256
F32, BF16 = jnp.float32, jnp.bfloat16


def collective_form(gate_pre, up_pre, down_weight, residual):
    hidden = (jax.nn.silu(gate_pre.astype(F32)) * up_pre.astype(F32)).astype(BF16)
    every_token = jnp.dot(
        lax.all_gather(hidden, "tok", axis=0, tiled=True),
        down_weight,
        preferred_element_type=F32,
    )
    partial_value = lax.all_to_all(every_token, "tok", split_axis=0, concat_axis=1, tiled=True)
    summed = lax.psum_scatter(partial_value, "hid", scatter_dimension=1, tiled=True)
    return (summed + residual.astype(F32)).astype(BF16)


def kernel(
    gate, up, weight, out,
    gbuf, ubuf, wbuf, hown, hrem,
    acc_o, ysend_o, yrecv_o, zsend_o, zrecv_o, fsend_o,
    acc_r, ysend_r, yrecv_r, zsend_r, zrecv_r, fsend_r, land,
    gsem, usem, wsem, xs, xr, cs, cr, ls, lr, ys, yr, zs, zr, fs, fr,
):
    nk, rows, ff = gbuf.shape
    nt, _, tile = acc_o.shape
    half, tokens = nt * tile, nk * rows
    t, h = lax.axis_index("tok"), lax.axis_index("hid")
    x, c = lax.div(t, 2), lax.rem(t, 2)
    z, y = lax.div(h, 2), lax.rem(h, 2)
    z1, z0 = lax.div(z, 2), lax.rem(z, 2)
    gathers = z0 == c
    passes = jnp.logical_not(gathers)
    core_t, x_t = 2 * x + 1 - c, 2 * (1 - x) + c
    y_h, z_h = 2 * z + 1 - y, 2 * (2 * z1 + 1 - z0) + y

    def load(k, source, buf, sem):
        return pltpu.make_async_copy(source.at[pl.ds(k * rows, rows)], buf.at[k], sem.at[k])

    def load_weight(n):
        start = jnp.where(n < nt, (1 - y) * half + n * tile, y * half + (n - nt) * tile)
        columns = pl.ds(pl.multiple_of(start, tile), tile)
        return pltpu.make_async_copy(weight.at[:, columns], wbuf.at[n], wsem.at[n])

    def remote(src, dst, send, recv, tok, hid):
        return pltpu.make_async_remote_copy(
            src_ref=src, dst_ref=dst, send_sem=send, recv_sem=recv,
            device_id=(tok, hid), device_id_type=MESH,
        )

    def own(k, core):
        return hown.at[pl.ds(pl.multiple_of(core * tokens + k * rows, rows), rows)]

    def rem(k, core):
        return hrem.at[k, pl.ds(pl.multiple_of(core * rows, rows), rows)]

    def core_copy(k, core):
        return remote(own(k, core), own(k, core), cs.at[k], cr.at[k], core_t, h)

    def x_copy(k):
        return remote(own(k, c), rem(k, c), xs.at[k], xr.at[k], x_t, h)

    def relay(k, core):
        return remote(rem(k, core), rem(k, core), ls.at[k], lr.at[k], core_t, h)

    class Own:
        index, acc = nk, acc_o
        ysend, yrecv, zsend, zrecv, fsend = ysend_o, yrecv_o, zsend_o, zrecv_o, fsend_o
        chip, first, count = x, 0, tokens

        def hidden():
            return hown[...]

    def remote_chunk(k):
        class Rem:
            index, acc = k, acc_r.at[k]
            ysend, yrecv, zsend = ysend_r.at[k], yrecv_r.at[k], zsend_r.at[k]
            zrecv, fsend = zrecv_r.at[k], fsend_r.at[k]
            chip, first, count = 1 - x, pl.multiple_of(k * rows, rows), rows

            def hidden():
                return hrem[k]

        return Rem

    def y_copy(g, n):
        i = g.index
        return remote(g.ysend.at[n], g.yrecv.at[n], ys.at[i, n], yr.at[i, n], t, y_h)

    def z_copy(g, n):
        i = g.index
        return remote(g.zsend.at[n], g.zrecv.at[n], zs.at[i, n], zr.at[i, n], t, z_h)

    def final_copy(g, n, core, slot, tok):
        return remote(
            g.fsend.at[n, pl.ds(core * g.count, g.count)],
            land.at[slot, n, pl.ds(g.first, g.count)],
            fs.at[g.index, n, core], fr.at[slot, g.index, n], tok, 2 * t + y,
        )

    def each(count, step):
        def one(n, _):
            step(n)
            return 0

        lax.fori_loop(0, count, one, 0)

    for k in range(nk):
        load(k, gate, gbuf, gsem).start()
        load(k, up, ubuf, usem).start()
    for n in range(2 * nt):
        load_weight(n).start()

    barrier = pltpu.get_barrier_semaphore()

    def greet(tok, hid):
        pl.semaphore_signal(barrier, inc=1, device_id=(tok, hid), device_id_type=MESH)

    greet(core_t, h)
    greet(x_t, h)
    greet(t, y_h)

    @pl.when(gathers)
    def _():
        greet(t, z_h)

    source_h = [2 * (2 * slot + z0) + y for slot in range(2)]
    foreign = [jnp.logical_or(z != t, z1 != slot) for slot in range(2)]
    for slot in range(2):

        @pl.when(foreign[slot])
        def _():
            greet(z, source_h[slot])

    owners = jnp.where(z == t, 3, 4)
    pl.semaphore_wait(barrier, 3 + jnp.where(gathers, owners, 1))

    wide = 512

    def activate(k):
        load(k, gate, gbuf, gsem).wait()
        load(k, up, ubuf, usem).wait()

        def piece(j):
            columns = pl.ds(pl.multiple_of(j * wide, wide), wide)
            v = gbuf[k, :, columns].astype(F32)
            u = ubuf[k, :, columns].astype(F32)
            own(k, c)[:, columns] = (v / (1.0 + jnp.exp(-v)) * u).astype(BF16)

        each(ff // wide, piece)
        x_copy(k).start()
        core_copy(k, c).start()

    each(nk, activate)

    def multiply(g, first_use):
        def give(n):
            if first_use:
                load_weight(n).wait()
            g.ysend[n] = jnp.dot(g.hidden(), wbuf[n], preferred_element_type=F32).astype(BF16)
            y_copy(g, n).start()

        def keep(n):
            if first_use:
                load_weight(nt + n).wait()
            g.acc[n] = jnp.dot(g.hidden(), wbuf[nt + n], preferred_element_type=F32)

        each(nt, give)
        each(nt, keep)

    def after_y(g, n):
        y_copy(g, n).wait_recv()

        @pl.when(gathers)
        def _():
            g.acc[n] = g.acc[n] + g.yrecv[n].astype(F32)

        @pl.when(passes)
        def _():
            g.zsend[n] = (g.acc[n] + g.yrecv[n].astype(F32)).astype(BF16)
            z_copy(g, n).start()

    def is_local(g, core):
        tok = 2 * g.chip + core
        return tok, jnp.logical_and(tok == t, z == t)

    def after_z(g, n):
        @pl.when(gathers)
        def _():
            z_copy(g, n).wait_recv()
            g.fsend[n] = (g.acc[n] + g.zrecv[n].astype(F32)).astype(BF16)
            for core in range(2):
                tok, local = is_local(g, core)
                if g is Own:

                    @pl.when(local)
                    def _():
                        land[z1, n] = g.fsend[n, core * tokens : (core + 1) * tokens]

                    @pl.when(jnp.logical_not(local))
                    def _():
                        final_copy(g, n, core, z1, tok).start()

                else:
                    final_copy(g, n, core, z1, tok).start()

    for k in range(nk):
        core_copy(k, 1 - c).wait_recv()
    multiply(Own, True)
    after_y(Own, 0)

    def chunk(i):
        @pl.when(i < nk)
        def _():
            x_copy(i).wait_recv()
            relay(i, c).start()
            relay(i, 1 - c).wait_recv()
            multiply(remote_chunk(i), False)

        @pl.when(i + 1 < nt)
        def _():
            after_y(Own, i + 1)

        @pl.when(i < nt)
        def _():
            after_z(Own, i)

        @pl.when(jnp.logical_and(i >= 1, i <= nk))
        def _():
            g = remote_chunk(i - 1)
            each(nt, lambda n: after_y(g, n))

        @pl.when(i >= 2)
        def _():
            g = remote_chunk(i - 2)
            each(nt, lambda n: after_z(g, n))

    each(max(nk + 2, nt), chunk)

    def finish(first, count, index):
        for n in range(nt):
            for slot in range(2):

                @pl.when(foreign[slot])
                def _():
                    piece = land.at[slot, n, pl.ds(first, count)]
                    arrival = fr.at[slot, index, n]
                    remote(piece, piece, fs.at[0, 0, 0], arrival, core_t, h).wait_recv()

            out[pl.ds(first, count), n * tile : (n + 1) * tile] = land[
                0, n, pl.ds(first, count)
            ].astype(F32) + land[1, n, pl.ds(first, count)].astype(F32)

    @pl.when(z1 == x)
    def _():
        finish(0, tokens, nk)

    @pl.when(z1 != x)
    def _():
        each(nk, lambda k: finish(pl.multiple_of(k * rows, rows), rows, k))

    def drain_k(k):
        x_copy(k).wait_send()
        core_copy(k, c).wait_send()
        relay(k, c).wait_send()

    each(nk, drain_k)

    def drain(g):
        def step(n):
            y_copy(g, n).wait_send()

            @pl.when(passes)
            def _():
                z_copy(g, n).wait_send()

            @pl.when(gathers)
            def _():
                for core in range(2):
                    tok, local = is_local(g, core)

                    @pl.when(jnp.logical_not(local))
                    def _():
                        final_copy(g, n, core, z1, tok).wait_send()

        each(nt, step)

    drain(Own)
    each(nk, lambda k: drain(remote_chunk(k)))


def kernel_form(gate_pre, up_pre, down_weight, residual):
    tokens, ff = gate_pre.shape
    half = residual.shape[1]
    rows, nk, nt = ROWS, tokens // ROWS, half // TILE
    dma = pltpu.SemaphoreType.DMA
    summed = pl.pallas_call(
        kernel,
        out_shape=jax.ShapeDtypeStruct((tokens, half), F32),
        in_specs=[pl.BlockSpec(memory_space=pl.ANY)] * 3,
        out_specs=pl.BlockSpec(memory_space=pltpu.VMEM),
        scratch_shapes=[
            pltpu.VMEM((nk, rows, ff), BF16),
            pltpu.VMEM((nk, rows, ff), BF16),
            pltpu.VMEM((2 * nt, ff, TILE), BF16),
            pltpu.VMEM((2 * tokens, ff), BF16),
            pltpu.VMEM((nk, 2 * rows, ff), BF16),
            pltpu.VMEM((nt, 2 * tokens, TILE), F32),
        ]
        + [pltpu.VMEM((nt, 2 * tokens, TILE), BF16)] * 5
        + [pltpu.VMEM((nk, nt, 2 * rows, TILE), F32)]
        + [pltpu.VMEM((nk, nt, 2 * rows, TILE), BF16)] * 5
        + [pltpu.VMEM((2, nt, tokens, TILE), BF16)]
        + [dma((nk,)), dma((nk,)), dma((2 * nt,))]
        + [dma((nk,))] * 6
        + [dma((nk + 1, nt))] * 4
        + [dma((nk + 1, nt, 2)), dma((2, nk + 1, nt))],
        compiler_params=pltpu.CompilerParams(
            collective_id=0, has_side_effects=True, vmem_limit_bytes=50 * 2**20
        ),
        cost_estimate=pl.CostEstimate(
            flops=2 * 4 * tokens * ff * 2 * half,
            bytes_accessed=2 * ff * (2 * half + 2 * tokens),
            transcendentals=tokens * ff,
        ),
    )(gate_pre, up_pre, down_weight)
    return (summed + residual.astype(F32)).astype(BF16)


def solution(mesh):
    in_specs = (P("tok", "hid"), P("tok", "hid"), P("hid", "tok"), P("tok", "hid"))
    out_specs = P("tok", "hid")
    fits = mesh.shape["tok"] == 4 and mesh.shape["hid"] == 8
    return jax.shard_map(
        kernel_form if fits else collective_form,
        mesh=mesh, in_specs=in_specs, out_specs=out_specs, check_vma=False,
    )
```

time: 174 us -> 45.2 us (0.26)
  waiting for transfers between devices: 106 us -> 0 us
  Pallas kernels: 0 us -> 42 us
  blocking collectives: 39.4 us -> 0 us
  between operations: 13.4 us -> 0.02 us
  matrix products: 8.56 us -> 0 us
  other arithmetic: 4.42 us -> 0.71 us
    reduce_scatter x1 -> x0, waiting for transfers between devices: 74.6 us -> none  [hidden_total(): lax.psum_scatter(partial_value, 'hid', scatter_dimension=1, tiled=True)]
    pallas_call x0 -> x1, Pallas kernels: none -> 42 us  [kernel_form(): pl.pallas_call(kernel, out_shape=jax.ShapeDtypeStruct((tokens, half), F32...]
    all_to_all x1 -> x0, blocking collectives: 39.4 us -> none  [per_device(): lax.all_to_all(every_token, 'tok', split_axis=0, concat_axis=1, tiled=True)]
    all_gather x1 -> x0, waiting for transfers between devices: 31.3 us -> none  [per_device(): lax.all_gather(hidden, 'tok', axis=0, tiled=True)]
    dot_general x1 -> x0, matrix products: 8.56 us -> none  [per_device(): jnp.dot(lax.all_gather(hidden, 'tok', axis=0, tiled=True), down_weight, p...]
    convert_element_type x2 -> x1, other arithmetic: 4.42 us -> 0.71 us  [kernel_form(): return (summed + residual.astype(F32)).astype(BF16)]
    unnamed x2 -> x6, local copies, waits for them, and re-layouts: 0.01 us -> 2.27 us
    all_to_all x1 -> x0, local copies, waits for them, and re-layouts: 1.85 us -> none  [per_device(): lax.all_to_all(every_token, 'tok', split_axis=0, concat_axis=1, tiled=True)]
  transfers between devices with their start and end apart: 2 -> 0, of which waited for: 2 -> 0; matrix products, arithmetic and copies ran while one was open for 0% -> 0% of each run, Pallas kernels for 0% -> 0%
where the time goes in v2:
time: 45.2 us; the launch traced here: 45 us
  Pallas kernels  42 us (93%)
  local copies, waits for them, and re-layouts  2.27 us (5%)
  other arithmetic  0.71 us (2%)
    pallas_call x1, Pallas kernels, kernel_form(): pl.pallas_call(kernel, out_shape=jax.ShapeDtypeStruct((tokens, half), F32...  42 us
    unnamed x6, local copies, waits for them, and re-layouts  2.27 us

profile of v2, /device:TPU:0, one launch (start us, length us, event | category | flops | bytes accessed | tf_op | source)
XLA Modules:
  0.0 45.0 jit_solution(4584827694377288396)
XLA Ops:
  0.0 0.0 copy-start
  0.0 1.1 %copy-done = bf16[128,3072]{1,0:T(8,128)(2,1)S(1)} copy-done((bf16[128,3072]{1,0:T(8,128)(2,1)S(1)}, bf16[128,3072]{1,0:T(8,128)(2,1)}, u32[]{:S(2)}) %copy-start) | copy-done | bytes 786456
  1.1 0.0 copy-start.1
  1.1 1.1 %copy-done.1 = bf16[128,3072]{1,0:T(8,128)(2,1)S(1)} copy-done((bf16[128,3072]{1,0:T(8,128)(2,1)S(1)}, bf16[128,3072]{1,0:T(8,128)(2,1)}, u32[]{:S(2)}) %copy-start.1) | copy-done | bytes 786456
  2.3 0.0 copy-start.2
  2.3 42.0 %shard_map.46 = f32[128,768]{1,0:T(8,128)S(1)} custom-call(bf16[128,3072]{1,0:T(8,128)(2,1)S(1)} %copy-done, bf16[128,3072]{1,0:T(8,128)(2,1)S(1)} %copy-done.1, bf16[3072,1536]{1,0:T(8,128)(2,1)} %weight.1), custom_call_target="tpu_custom_call" | custom-call | flops 4831838208 | bytes 11010048 | tf_op jit(solution)/shard_map/pallas_call | solution.py:305
  44.3 0.0 copy-done.2
  44.3 0.7 %add_convert_fusion = bf16[128,768]{1,0:T(8,128)(2,1)} fusion(f32[128,768]{1,0:T(8,128)S(1)} %shard_map.46, bf16[128,768]{1,0:T(8,128)(2,1)S(1)} %copy-done.2), kind=kLoop, calls=%fused_computation | loop fusion | flops 294912 | bytes 786432 | tf_op jit(solution)/shard_map/convert_element_type | solution.py:335
Async XLA Ops:
  0.0 1.1 %copy-start = (bf16[128,3072]{1,0:T(8,128)(2,1)S(1)}, bf16[128,3072]{1,0:T(8,128)(2,1)}, u32[]{:S(2)}) copy-start(bf16[128,3072]{1,0:T(8,128)(2,1)} %gate.1) | copy-start | bytes 2359300
  1.1 1.1 %copy-start.1 = (bf16[128,3072]{1,0:T(8,128)(2,1)S(1)}, bf16[128,3072]{1,0:T(8,128)(2,1)}, u32[]{:S(2)}) copy-start(bf16[128,3072]{1,0:T(8,128)(2,1)} %up.1) | copy-start | bytes 2359300
  2.3 42.0 %copy-start.2 = (bf16[128,768]{1,0:T(8,128)(2,1)S(1)}, bf16[128,768]{1,0:T(8,128)(2,1)}, u32[]{:S(2)}) copy-start(bf16[128,768]{1,0:T(8,128)(2,1)} %param.7) | copy-start | bytes 589828
